TPU v7x, 256 devices: a whole 4x4x8 slice. The times are simulated.
256 devices in a mesh: gx: 16 (over y, x), gy: 16 (over z, core).
Axes of the slice: x: 4, y: 4, z: 8, core: 2. Of those that a mesh axis runs over, the one named last changes fastest.
Arguments:
- pressure: float32 [2, 2048, 2048], P(None, 'gx', 'gy'), may hold values from 0.5 to 1.5
- saturations: float32 [2, 2, 2048, 2048], P(None, None, 'gx', 'gy'), may hold values from 0.05 to 0.4
- old_mass: float32 [3, 2, 2048, 2048], P(None, None, 'gx', 'gy'), may hold values from 0 to 0.4
- pore_volume: float32 [2, 2048, 2048], P(None, 'gx', 'gy'), may hold values from 0.3 to 3
- transmissibility: float32 [3, 2, 2048, 2048], P(None, None, 'gx', 'gy'), may hold values from 0.3 to 3
- direction: float32 [3, 2, 2048, 2048], P(None, None, 'gx', 'gy'), may hold values from -6 to 6
- seg_pressure: float32 [512, 128], P('gx'), may hold values from 0.4 to 1.2
- seg_direction: float32 [512, 128], P('gx'), may hold values from -6 to 6
- perf_cell: int32 [512, 128], P('gx'), may hold values from 0 to 524287, as said below
- well_index: float32 [512, 128], P('gx'), may hold values from 0.2 to 2
- parent: int32 [512, 128], P('gx'), may hold values from 0 to 126, as said below
- seg_head: float32 [512, 128], P('gx'), may hold values from 0 to 0.3
- well_mode: int32 [512], P('gx'), may hold values from 0 to 1
- bhp_limit: float32 [512], P('gx'), may hold values from 0.3 to 0.8
- guide_rate: float32 [512], P('gx'), may hold values from 0.5 to 5
- group_of: int32 [512, 1], P('gx'), may hold values from 0 to 127
- group_target: float32 [128], replicated, may hold values from 200 to 800
Outputs:
- cell_residual: float32 [3, 2, 2048, 2048], P(None, None, 'gx', 'gy')
- cell_jvp: float32 [3, 2, 2048, 2048], P(None, None, 'gx', 'gy')
- seg_residual: float32 [512, 128], P(('gx', 'gy'))
- seg_jvp: float32 [512, 128], P(('gx', 'gy'))
- group_rates: float32 [3, 128], replicated
Inputs may be any that keep to these rules, and one draw needn't show every extreme that they name: perf_cell codes (layer * 128 + xl) * 2048 + row, with xl the column within the strip of 128 columns of the well's block of 32 wells. `parent`: segment 0 of every well names itself; every other segment names a segment of lower number. `group_of`: every group has at least one well.
All inputs are finite; a program needn't handle non-finite values.
Results may differ from a plain program's by a relative error of at most 0.0003.
Values sent between devices are 32-bit elements; how exact they have to be, the bound alone decides.
A program may use at most 128 MiB of HBM per device.

v0:
```python
import jax
import jax.numpy as jnp
from jax import lax
from jax.sharding import PartitionSpec as P

COMPRESS = (0.05, 0.2, 1.0)
VISCOSITY = (0.5, 1.0, 0.2)
DENSITY = (1.0, 0.8, 0.2)
ROCK_COMP = 0.01
GRAVITY = 0.05
UPWIND_WIDTH = 0.02
FRICTION = 0.002
RATE_SCALE = 0.1


def padded_2(x, sides, width):
    for axis, dim in sides:
        devices, length = (lax.axis_size(axis), x.shape[dim])
        up = [(i, (i + 1) % devices) for i in range(devices - 1)]
        down = [(j, i) for i, j in up]
        last = lax.slice_in_dim(x, length - width, length, axis=dim)
        first = lax.slice_in_dim(x, 0, width, axis=dim)
        before = lax.ppermute(last, axis, up)
        after = lax.ppermute(first, axis, down)
        x = jnp.concatenate([before, x, after], axis=dim)
    return x


def phase_props(press, water, gas):
    oil = 1.0 - water - gas
    satur = (water, oil, gas)
    rock = 1.0 + ROCK_COMP * (press - 1.0)
    mobility = []
    masses = []
    for phase in range(3):
        volume = jnp.exp(COMPRESS[phase] * (press - 1.0))
        mobility.append(satur[phase] * satur[phase] * volume / VISCOSITY[phase])
        masses.append(rock * satur[phase] * volume)
    return (jnp.stack(mobility), jnp.stack(masses))


def face_flux(press_in, press_out, mobil_in, mobil_out, trans, lift):
    fluxes = []
    for phase in range(3):
        potential = press_in - press_out + DENSITY[phase] * lift
        upwind = jax.nn.sigmoid(potential / UPWIND_WIDTH)
        fluxes.append(
            trans * (upwind * mobil_in[phase] + (1.0 - upwind) * mobil_out[phase]) * potential
        )
    return jnp.stack(fluxes)


def ancestry(parent):
    count = parent.shape[1]
    segment_ids = jnp.arange(count, dtype=jnp.int32)
    reach = (segment_ids[None, :, None] == segment_ids[None, None, :]) | (
        parent[:, None, :] == segment_ids[None, :, None]
    )
    reach = reach.astype(jnp.bfloat16)
    for level in range((count - 1).bit_length()):
        product = jnp.einsum("wsu,wut->wst", reach, reach, preferred_element_type=jnp.float32)
        reach = jnp.minimum(product, 1.0).astype(jnp.bfloat16)
    return reach.astype(jnp.float32)


def segment_terms(parent, seg_head, well_mode, bhp_limit, target):
    reach = ancestry(parent)

    def equations(total_vals, seg_vals):
        flow = jnp.einsum("wst,wt->ws", reach, total_vals, precision=lax.Precision.HIGHEST)
        above = jnp.take_along_axis(seg_vals, parent, axis=1)
        inner = seg_vals - above - seg_head - FRICTION * flow
        root = jnp.where(
            well_mode == 1, RATE_SCALE * (flow[:, 0] - target), seg_vals[:, 0] - bhp_limit
        )
        return inner.at[:, 0].set(root)

    return equations


def per_device(
    pressure,
    saturations,
    old_mass,
    pore_volume,
    transmissibility,
    direction,
    seg_pressure,
    seg_direction,
    perf_cell,
    well_index,
    parent,
    seg_head,
    well_mode,
    bhp_limit,
    guide_rate,
    group_of,
    group_target,
):
    layers, cols, rows = pressure.shape
    col_count = lax.axis_size("gx")
    row_count = lax.axis_size("gy")
    col_index = lax.axis_index("gx")
    row_index = lax.axis_index("gy")
    col_glob = col_index * cols + jnp.arange(cols, dtype=jnp.int32)
    row_glob = row_index * rows + jnp.arange(rows, dtype=jnp.int32)
    trans_cols = jnp.where(
        (col_glob == cols * col_count - 1)[None, :, None], 0.0, transmissibility[0]
    )
    trans_rows = jnp.where(
        (row_glob == rows * row_count - 1)[None, None, :], 0.0, transmissibility[1]
    )
    stacked = jnp.concatenate(
        [pressure[None], saturations, direction, trans_cols[None], trans_rows[None]], axis=0
    )
    padded = padded_2(stacked, (("gx", 2), ("gy", 3)), 1)
    state_pad = padded[0:3]
    direc_pad = padded[3:6]
    tcol_pad = padded[6]
    trow_pad = padded[7]
    all_rows = rows * row_count
    layer_span = cols * all_rows
    layer = perf_cell // layer_span
    remain = perf_cell % layer_span
    local_row = remain % all_rows - row_index * rows
    owned = (local_row >= 0) & (local_row < rows)
    flat_cell = (layer * cols + remain // all_rows) * rows + jnp.clip(local_row, 0, rows - 1)
    weight = jnp.where(owned, well_index, 0.0)

    def local_terms(state, seg_vals):
        press = state[0]
        mobility, masses = phase_props(press, state[1], state[2])
        mobil_in = mobility[:, :, 1:-1, 1:-1]
        press_in = press[:, 1:-1, 1:-1]
        residual = masses[:, :, 1:-1, 1:-1] * pore_volume - old_mass
        flux_cols = face_flux(
            press[:, :-1, 1:-1],
            press[:, 1:, 1:-1],
            mobility[:, :, :-1, 1:-1],
            mobility[:, :, 1:, 1:-1],
            tcol_pad[:, :-1, 1:-1],
            0.0,
        )
        residual = residual + flux_cols[:, :, 1:] - flux_cols[:, :, :-1]
        flux_rows = face_flux(
            press[:, 1:-1, :-1],
            press[:, 1:-1, 1:],
            mobility[:, :, 1:-1, :-1],
            mobility[:, :, 1:-1, 1:],
            trow_pad[:, 1:-1, :-1],
            0.0,
        )
        residual = residual + flux_rows[:, :, :, 1:] - flux_rows[:, :, :, :-1]
        flux_layers = face_flux(
            press_in[:-1],
            press_in[1:],
            mobil_in[:, :-1],
            mobil_in[:, 1:],
            transmissibility[2][:-1],
            GRAVITY,
        )
        residual = (
            residual
            + jnp.pad(flux_layers, ((0, 0), (0, 1), (0, 0), (0, 0)))
            - jnp.pad(flux_layers, ((0, 0), (1, 0), (0, 0), (0, 0)))
        )
        mobil_flat = mobil_in.reshape(3, -1)
        rates = weight * mobil_flat[:, flat_cell] * (press_in.reshape(-1)[flat_cell] - seg_vals)
        residual = (
            residual.reshape(3, -1)
            .at[:, flat_cell.reshape(-1)]
            .add(rates.reshape(3, -1))
            .reshape(residual.shape)
        )
        return (residual, rates)

    primal, tangent = jax.jvp(local_terms, (state_pad, seg_pressure), (direc_pad, seg_direction))
    cell_residual, rates = primal
    cell_jvp, rate_tangent = tangent
    rate_total = jnp.sum(rates, axis=0)
    total_tangent = jnp.sum(rate_tangent, axis=0)
    member = (
        group_of[:, 0][:, None] == jnp.arange(group_target.shape[0], dtype=jnp.int32)[None, :]
    ).astype(jnp.float32)
    rates_part = jnp.dot(jnp.sum(rates, axis=2), member, precision=lax.Precision.HIGHEST)
    guide_part = jnp.dot(guide_rate, member, precision=lax.Precision.HIGHEST)
    guide_total = lax.psum(guide_part, "gx")
    group_rates = lax.psum(rates_part, ("gx", "gy"))
    target = (
        jnp.dot(member, group_target, precision=lax.Precision.HIGHEST)
        * guide_rate
        / jnp.dot(member, guide_total, precision=lax.Precision.HIGHEST)
    )
    well_count = seg_pressure.shape[0]
    share = well_count // row_count
    start = row_index * share

    def pick(values):
        return lax.dynamic_slice_in_dim(values, start, share, 0)

    total_sum, tangent_sum = lax.psum((rate_total, total_tangent), "gy")
    equations = segment_terms(parent, seg_head, well_mode, bhp_limit, target)
    seg_full, seg_tan = jax.jvp(equations, (total_sum, seg_pressure), (tangent_sum, seg_direction))
    seg_residual = pick(seg_full)
    seg_jvp = pick(seg_tan)
    return (cell_residual, cell_jvp, seg_residual, seg_jvp, group_rates)


def solution(mesh):
    placed = (
        P(None, "gx", "gy"),
        P(None, None, "gx", "gy"),
        P(None, None, "gx", "gy"),
        P(None, "gx", "gy"),
        P(None, None, "gx", "gy"),
        P(None, None, "gx", "gy"),
        P("gx", None),
        P("gx", None),
        P("gx", None),
        P("gx", None),
        P("gx", None),
        P("gx", None),
        P("gx"),
        P("gx"),
        P("gx"),
        P("gx", None),
        P(),
    )
    return jax.shard_map(
        per_device,
        mesh=mesh,
        in_specs=placed,
        out_specs=(
            P(None, None, "gx", "gy"),
            P(None, None, "gx", "gy"),
            P(("gx", "gy"), None),
            P(("gx", "gy"), None),
            P(),
        ),
        check_vma=False,
    )
```

profile of v0, /device:TPU:1, one launch (start us, length us, event | category | flops | bytes accessed | tf_op | source)
XLA Modules:
  0.0 510.7 jit_solution(14686973665699037031)
XLA Ops:
  2.6 1.0 constant_dynamic-update-slice_fusion
  3.7 1.0 select_dynamic-update-slice_fusion.1
  5.6 1.3 collective-permute-start.1
  6.9 4.6 collective-permute-start
  14.0 1.0 minimum_convert_fusion.2
  15.0 2.0 minimum_convert_fusion
  17.2 32.3 %psum.29 = f32[128]{0:T(128)S(1)} all-reduce(f32[128]{0:T(128)S(1)} %convolution_bitcast_fusion.1), channel_id=1, replica_groups=mesh['gx'=16,'gy'=16] {'gx'}, use_global_device_ids=true, to_apply=%region_5.6 | all-reduce | flops 128 | bytes 1024 | tf_op jit(solution)/shard_map/psum | solution.py:187
  51.9 9.9 %collective-permute-start.3 = (f32[8,2,130,1]{2,0,3,1:T(8,128)S(1)}, f32[8,2,130,1]{2,0,3,1:T(8,128)S(1)}, u32[]{:S(2)}, u32[]{:S(2)}) collective-permute-start(f32[8,2,130,1]{2,0,3,1:T(8,128)S(1)} %copy.106), channel_id=1, source_target_pairs={{1,0},{2,1},{3,2},{4,3},{5,4},{6,5},{7,6},{8,7},{9,8},{10,9},{11,1... | collective-permute-start | bytes 24968 | tf_op jit(solution)/shard_map/ppermute | solution.py:24
  62.4 3.6 collective-permute-start.2
  66.2 43.2 %gather_fusion.5 = f32[4096]{0:T(1024)} fusion(f32[32,128]{1,0:T(8,128)S(1)} %copy-done.1, s32[4096]{0:T(1024)S(1)} %fusion.156), kind=kCustom, calls=%fused_computation.5 | custom fusion | bytes 65536 | tf_op jit(solution)/shard_map/jvp(jit(take_along_axis))/gather | solution.py:71
  109.4 25.6 %gather_fusion.4 = f32[4096]{0:T(1024)S(1)} fusion(f32[32,128]{1,0:T(8,128)S(1)} %copy-done.2, s32[4096]{0:T(1024)S(1)} %fusion.156), kind=kCustom, calls=%fused_computation.4 | custom fusion | bytes 65536 | tf_op jit(solution)/shard_map/jvp(jit(take_along_axis))/gather | solution.py:71
  136.5 1.0 pad_maximum_fusion
  138.1 1.2 fusion.39
  143.0 1.0 pad_maximum_fusion.2
  145.2 8.6 %copy.109 = f32[3,2,128,128]{0,3,2,1:T(8,128)} copy(f32[3,2,128,128]{3,2,1,0:T(8,128)S(1)} %fusion.34) | data formatting | bytes 786432 | tf_op jit(solution)/shard_map/jvp()/sub | solution.py:163
  153.7 8.5 %copy.110 = f32[3,2,128,128]{0,3,2,1:T(8,128)} copy(f32[3,2,128,128]{3,2,1,0:T(8,128)S(1)} %get-tuple-element.106) | data formatting | bytes 786432 | tf_op jit(solution)/shard_map/jvp()/slice | solution.py:133
  162.2 16.5 %gather_fusion = f32[4096,3]{1,0:T(8,128)S(1)} fusion(f32[3,32768]{0,1:T(8,128)} %bitcast.414, s32[4096]{0:T(1024)S(1)} %get-tuple-element.69), kind=kCustom, calls=%fused_computation | custom fusion | bytes 114688 | tf_op jit(solution)/shard_map/jvp()/gather | solution.py:168
  178.8 40.6 %gather_fusion.3 = f32[4096]{0:T(1024)} fusion(f32[32768]{0:T(1024)S(1)} %bitcast.407, s32[4096]{0:T(1024)S(1)} %get-tuple-element.69), kind=kCustom, calls=%fused_computation.3 | custom fusion | bytes 49152 | tf_op jit(solution)/shard_map/jvp()/gather | solution.py:168
  219.4 23.0 %gather_fusion.1 = f32[4096]{0:T(1024)S(1)} fusion(f32[32768]{0:T(1024)S(1)} %bitcast.408, s32[4096]{0:T(1024)S(1)} %get-tuple-element.69), kind=kCustom, calls=%fused_computation.1 | custom fusion | bytes 49152 | tf_op jit(solution)/shard_map/jvp()/gather | solution.py:168
  242.4 36.5 %scatter_custom_fusion = f32[3,32768]{0,1:T(8,128)} fusion(f32[3,32768]{0,1:T(8,128)} %bitcast.409, s32[4096]{0:T(1024)} %bitcast.429, f32[4096,3]{1,0:T(8,128)S(1)} %gather_fusion, f32[4096]{0:T(1024)S(1)} %bitcast.419, f32[4096]{0:T(1024)S(1)} %bitcast.417), kind=kCustom, calls=%fused_computation.15 | custom fusion | flops 36864 | bytes 475136 | tf_op jit(solution)/shard_map/jvp()/scatter-add | solution.py:172
  278.9 10.7 %copy.115 = f32[3,2,128,128]{3,2,1,0:T(8,128)} copy(f32[3,2,128,128]{0,3,2,1:T(8,128)} %bitcast.410) | data formatting | bytes 786432
  289.6 2.5 fusion.31
  292.1 9.5 %copy.111 = f32[3,2,128,128]{0,3,2,1:T(8,128)} copy(f32[3,2,128,128]{3,2,1,0:T(8,128)} %fusion.31) | data formatting | bytes 786432 | tf_op jit(solution)/shard_map/jvp()/sub | solution.py:163
  301.6 8.5 %copy.112 = f32[3,2,128,128]{0,3,2,1:T(8,128)} copy(f32[3,2,128,128]{3,2,1,0:T(8,128)S(1)} %get-tuple-element.105) | data formatting | bytes 786432 | tf_op jit(solution)/shard_map/jvp()/slice | solution.py:133
  310.1 19.9 %gather_fusion.2 = f32[4096,3]{1,0:T(8,128)} fusion(f32[3,32768]{0,1:T(8,128)} %bitcast.415, s32[4096]{0:T(1024)S(1)} %get-tuple-element.69), kind=kCustom, calls=%fused_computation.2 | custom fusion | bytes 114688 | tf_op jit(solution)/shard_map/jvp()/gather | solution.py:168
  330.1 37.0 %scatter_custom_fusion.1 = f32[3,32768]{0,1:T(8,128)} fusion(f32[3,32768]{0,1:T(8,128)} %bitcast.411, s32[4096]{0:T(1024)} %bitcast.430, f32[4096,3]{1,0:T(8,128)} %gather_fusion.2, f32[4096,3]{1,0:T(8,128)S(1)} %gather_fusion, f32[4096]{0:T(1024)S(1)} %bitcast.425, f32[4096]{0:T(1024)S(1)} %bitcast.420, f32[4096]{0:T(1024)S(1)} %bitcast.418), kind=kCustom, calls=%fused_computation.13 | custom fusion | flops 73728 | bytes 2588672 | tf_op jit(solution)/shard_map/jvp()/scatter-add | solution.py:172
  367.0 10.6 %copy.116 = f32[3,2,128,128]{3,2,1,0:T(8,128)} copy(f32[3,2,128,128]{0,3,2,1:T(8,128)} %bitcast.412) | data formatting | bytes 786432
  377.7 4.6 add_reduce_fusion
  382.4 46.0 %all-reduce.4 = (f32[32,128]{1,0:T(8,128)S(1)}, f32[32,128]{1,0:T(8,128)S(1)}) all-reduce(f32[32,128]{1,0:T(8,128)S(1)} %get-tuple-element.55, f32[32,128]{1,0:T(8,128)S(1)} %get-tuple-element.54), channel_id=1, replica_groups=mesh['gx'=16,'gy'=16] {'gy'}, use_global_device_ids=true, to_apply=%region_3.4 | all-reduce | flops 8192 | bytes 65536 | tf_op jit(solution)/shard_map/psum | solution.py:201
  428.4 1.7 fusion.175
  430.2 1.7 fusion.174
  435.5 75.3 %psum.31 = f32[3,128]{1,0:T(4,128)} all-reduce(f32[3,128]{1,0:T(4,128)S(1)} %fusion.157), channel_id=1, replica_groups=mesh['gx'=16,'gy'=16] {'gx','gy'}, use_global_device_ids=true, to_apply=%region_9.10 | all-reduce | flops 384 | bytes 3072 | tf_op jit(solution)/shard_map/psum | solution.py:188
  (105 shorter events, 19.0 us)
Async XLA Ops:
  0.6 431.5 %copy-start = (f32[128]{0:T(128)S(1)}, f32[128]{0:T(128)}, u32[]{:S(2)}) copy-start(f32[128]{0:T(128)} %param.37) | copy-start | bytes 1540
  0.6 10.9 %copy-start.8 = (s32[32,128]{1,0:T(8,128)S(1)}, s32[32,128]{1,0:T(8,128)}, u32[]{:S(2)}) copy-start(s32[32,128]{1,0:T(8,128)} %param.29) | copy-start | bytes 49156
  0.7 11.5 %copy-start.12 = (f32[32,128]{1,0:T(8,128)S(1)}, f32[32,128]{1,0:T(8,128)}, u32[]{:S(2)}) copy-start(f32[32,128]{1,0:T(8,128)} %param.30) | copy-start | bytes 49156
  0.7 11.5 %copy-start.9 = (s32[32,128]{1,0:T(8,128)S(1)}, s32[32,128]{1,0:T(8,128)}, u32[]{:S(2)}) copy-start(s32[32,128]{1,0:T(8,128)} %param.31) | copy-start | bytes 49156
  5.6 45.2 %collective-permute-start.1 = (f32[8,2,1,128]{3,2,1,0:T(1,128)S(1)}, f32[8,2,1,128]{3,2,1,0:T(1,128)S(1)}, u32[]{:S(2)}, u32[]{:S(2)}) collective-permute-start(f32[8,2,1,128]{3,2,1,0:T(1,128)S(1)} %get-tuple-element.89), channel_id=1, source_target_pairs={{16,0},{32,16},{48,32},{64,48},{80,64},{96,80},{112,96},{128,112},... | collective-permute-start | bytes 24584 | tf_op jit(solution)/shard_map/ppermute | solution.py:24
  6.9 43.9 %collective-permute-start = (f32[8,2,1,128]{3,2,1,0:T(1,128)S(1)}, f32[8,2,1,128]{3,2,1,0:T(1,128)S(1)}, u32[]{:S(2)}, u32[]{:S(2)}) collective-permute-start(f32[8,2,1,128]{3,2,1,0:T(1,128)S(1)} %get-tuple-element.88), channel_id=1, source_target_pairs={{0,16},{16,32},{32,48},{48,64},{64,80},{80,96},{96,112},{112,128},... | collective-permute-start | bytes 24584 | tf_op jit(solution)/shard_map/ppermute | solution.py:23
  15.0 2.0 copy-start.16
  15.0 2.0 copy-start.19
  15.0 35.2 %copy-start.2 = (f32[32,128]{1,0:T(8,128)S(1)}, f32[32,128]{1,0:T(8,128)}, u32[]{:S(2)}) copy-start(f32[32,128]{1,0:T(8,128)} %param.27) | copy-start | bytes 49156
  51.3 14.8 %copy-start.1 = (f32[32,128]{1,0:T(8,128)S(1)}, f32[32,128]{1,0:T(8,128)}, u32[]{:S(2)}) copy-start(f32[32,128]{1,0:T(8,128)} %param.28) | copy-start | bytes 49156
  51.9 83.8 %collective-permute-start.3 = (f32[8,2,130,1]{2,0,3,1:T(8,128)S(1)}, f32[8,2,130,1]{2,0,3,1:T(8,128)S(1)}, u32[]{:S(2)}, u32[]{:S(2)}) collective-permute-start(f32[8,2,130,1]{2,0,3,1:T(8,128)S(1)} %copy.106), channel_id=1, source_target_pairs={{1,0},{2,1},{3,2},{4,3},{5,4},{6,5},{7,6},{8,7},{9,8},{10,9},{11,1... | collective-permute-start | bytes 24968 | tf_op jit(solution)/shard_map/ppermute | solution.py:24
  62.4 73.7 %collective-permute-start.2 = (f32[8,2,130,1]{2,0,3,1:T(8,128)S(1)}, f32[8,2,130,1]{2,0,3,1:T(8,128)S(1)}, u32[]{:S(2)}, u32[]{:S(2)}) collective-permute-start(f32[8,2,130,1]{2,0,3,1:T(8,128)S(1)} %copy.105), channel_id=1, source_target_pairs={{0,1},{1,2},{2,3},{3,4},{4,5},{5,6},{6,7},{7,8},{8,9},{9,10},{10,1... | collective-permute-start | bytes 24968 | tf_op jit(solution)/shard_map/ppermute | solution.py:23
  140.7 1.2 copy-start.5
  143.0 1.8 copy-start.6
  143.0 1.8 copy-start.7
  219.4 23.0 %copy-start.11 = (f32[4096]{0:T(1024)S(1)}, f32[4096]{0:T(1024)}, u32[]{:S(2)}) copy-start(f32[4096]{0:T(1024)} %gather_fusion.3) | copy-start | bytes 49156
  278.9 10.7 %copy-start.4 = (f32[3,1,128,128]{3,2,1,0:T(8,128)S(1)}, f32[3,1,128,128]{3,2,1,0:T(8,128)}, u32[]{:S(2)}) copy-start(f32[3,1,128,128]{3,2,1,0:T(8,128)} %get-tuple-element.112) | copy-start | bytes 589828
  377.7 50.7 %copy-start.3 = (bf16[32,128,128]{2,1,0:T(8,128)(2,1)S(1)}, bf16[32,128,128]{2,1,0:T(8,128)(2,1)}, u32[]{:S(2)}) copy-start(bf16[32,128,128]{2,1,0:T(8,128)(2,1)} %minimum_convert_fusion) | copy-start | bytes 3145732
  377.7 52.5 %copy-start.10 = (f32[4096]{0:T(1024)S(1)}, f32[4096]{0:T(1024)}, u32[]{:S(2)}) copy-start(f32[4096]{0:T(1024)} %gather_fusion.5) | copy-start | bytes 49156
  382.3 49.8 %copy-start.14 = (f32[32]{0:T(128)S(1)}, f32[32]{0:T(128)}, u32[]{:S(2)}) copy-start(f32[32]{0:T(128)} %slice_reduce_fusion.2) | copy-start | bytes 388
  382.3 49.8 %copy-start.15 = (s32[32]{0:T(128)S(1)}, s32[32]{0:T(128)}, u32[]{:S(2)}) copy-start(s32[32]{0:T(128)} %param.33) | copy-start | bytes 388
  382.3 49.8 %copy-start.17 = (f32[32]{0:T(128)S(1)}, f32[32]{0:T(128)}, u32[]{:S(2)}) copy-start(f32[32]{0:T(128)} %param.35) | copy-start | bytes 388
  382.3 49.8 %copy-start.18 = (f32[32]{0:T(128)S(1)}, f32[32]{0:T(128)}, u32[]{:S(2)}) copy-start(f32[32]{0:T(128)} %param.34) | copy-start | bytes 388
  382.4 49.8 %copy-start.20 = (s32[32,1]{0,1:T(1,128)S(1)}, s32[32,1]{0,1:T(1,128)}, u32[]{:S(2)}) copy-start(s32[32,1]{0,1:T(1,128)} %param.36) | copy-start | bytes 388
  382.4 49.8 %copy-start.21 = (f32[32]{0:T(128)S(1)}, f32[32]{0:T(128)}, u32[]{:S(2)}) copy-start(f32[32]{0:T(128)} %convolution_bitcast_fusion) | copy-start | bytes 388
  382.4 50.1 %copy-start.13 = (f32[32,128]{1,0:T(8,128)S(1)}, f32[32,128]{1,0:T(8,128)}, u32[]{:S(2)}) copy-start(f32[32,128]{1,0:T(8,128)} %param.32) | copy-start | bytes 49156
where the time goes:
time: 512 us; the launch traced here: 511 us
  local copies, waits for them, and re-layouts  233 us (46%)
  blocking collectives  154 us (30%)
  other arithmetic  93.7 us (18%)
  starting transfers between devices  19.4 us (4%)
  matrix products  9.4 us (2%)
    psum x1, blocking collectives, per_device(): group_rates = lax.psum(rates_part, ('gx', 'gy'))  75.3 us
    scatter-add x2, other arithmetic, local_terms(): residual = residual.reshape(3, -1).at[:, flat_cell.reshape(-1)].add(rates...  73.5 us
    gather x2, local copies, waits for them, and re-layouts, equations(): above = jnp.take_along_axis(seg_vals, parent, axis=1)  68.8 us
    gather x2, local copies, waits for them, and re-layouts, local_terms(): press_in.reshape(-1)[flat_cell] - seg_vals  63.6 us
    psum x1, blocking collectives, per_device(): total_sum, tangent_sum = lax.psum((rate_total, total_tangent), 'gy')  46 us
    gather x2, local copies, waits for them, and re-layouts, local_terms(): mobil_flat[:, flat_cell]  36.5 us
    psum x1, blocking collectives, per_device(): guide_total = lax.psum(guide_part, 'gx')  32.3 us
    unnamed x49, local copies, waits for them, and re-layouts  24.4 us
  transfers between devices with their start and end apart: 4, of which 0 were waited for; matrix products, arithmetic and copies ran while one was open for 15% of the time, Pallas kernels for 0%

commit v1 on v0

--- a/solution.py
+++ b/solution.py
@@ -184,7 +184,7 @@
     ).astype(jnp.float32)
     rates_part = jnp.dot(jnp.sum(rates, axis=2), member, precision=lax.Precision.HIGHEST)
     guide_part = jnp.dot(guide_rate, member, precision=lax.Precision.HIGHEST)
-    guide_total = lax.psum(guide_part, "gx")
+    guide_total = jnp.sum(lax.all_gather(guide_part, "gx"), axis=0)
     group_rates = lax.psum(rates_part, ("gx", "gy"))
     target = (
         jnp.dot(member, group_target, precision=lax.Precision.HIGHEST)

time: 512 us -> 497 us (0.971)
  blocking collectives: 154 us -> 141 us
    psum x1 -> x0, blocking collectives: 32.3 us -> none  [per_device(): guide_total = lax.psum(guide_part, 'gx')]
    all_gather x0 -> x1, blocking collectives: none -> 18.6 us  [per_device(): guide_total = jnp.sum(lax.all_gather(guide_part, 'gx'), axis=0)]
  transfers between devices with their start and end apart: 4 -> 4, of which waited for: 0 -> 0; matrix products, arithmetic and copies ran while one was open for 15% -> 16% of each run, Pallas kernels for 0% -> 0%
where the time goes in v1:
time: 497 us; the launch traced here: 496 us
  local copies, waits for them, and re-layouts  233 us (47%)
  blocking collectives  141 us (28%)
  other arithmetic  93.7 us (19%)
  starting transfers between devices  17.2 us (3%)
  matrix products  9.4 us (2%)
    psum x1, blocking collectives, per_device(): group_rates = lax.psum(rates_part, ('gx', 'gy'))  76.6 us
    scatter-add x2, other arithmetic, local_terms(): residual = residual.reshape(3, -1).at[:, flat_cell.reshape(-1)].add(rates...  73.5 us
    gather x2, local copies, waits for them, and re-layouts, equations(): above = jnp.take_along_axis(seg_vals, parent, axis=1)  68.8 us
    gather x2, local copies, waits for them, and re-layouts, local_terms(): press_in.reshape(-1)[flat_cell] - seg_vals  63.6 us
    psum x1, blocking collectives, per_device(): total_sum, tangent_sum = lax.psum((rate_total, total_tangent), 'gy')  46 us
    gather x2, local copies, waits for them, and re-layouts, local_terms(): mobil_flat[:, flat_cell]  36.5 us
    unnamed x49, local copies, waits for them, and re-layouts  24.4 us
    all_gather x1, blocking collectives, per_device(): guide_total = jnp.sum(lax.all_gather(guide_part, 'gx'), axis=0)  18.6 us
  transfers between devices with their start and end apart: 4, of which 0 were waited for; matrix products, arithmetic and copies ran while one was open for 16% of the time, Pallas kernels for 0%

profile of v1, /device:TPU:1, one launch (start us, length us, event | category | flops | bytes accessed | tf_op | source)
XLA Modules:
  0.0 496.1 jit_solution(18124536446943893853)
XLA Ops:
  2.6 1.0 constant_dynamic-update-slice_fusion
  3.7 1.0 select_dynamic-update-slice_fusion.1
  5.6 1.3 collective-permute-start.1
  6.9 4.6 collective-permute-start
  14.0 1.0 minimum_convert_fusion.2
  15.0 2.0 minimum_convert_fusion
  17.2 18.6 %all-gather.1 = f32[16,1,128]{2,1,0:T(1,128)S(1)} all-gather(f32[1,1,128]{2,1,0:T(1,128)S(1)} %convolution_bitcast_fusion.1), channel_id=2, replica_groups=mesh['gx'=16,'gy'=16] {'gx'}, dimensions={0}, use_global_device_ids=true | all-gather | bytes 8704 | tf_op jit(solution)/shard_map/all_gather | solution.py:187
  38.2 7.7 %collective-permute-start.3 = (f32[8,2,130,1]{2,0,3,1:T(8,128)S(1)}, f32[8,2,130,1]{2,0,3,1:T(8,128)S(1)}, u32[]{:S(2)}, u32[]{:S(2)}) collective-permute-start(f32[8,2,130,1]{2,0,3,1:T(8,128)S(1)} %copy.106), channel_id=1, source_target_pairs={{1,0},{2,1},{3,2},{4,3},{5,4},{6,5},{7,6},{8,7},{9,8},{10,9},{11,1... | collective-permute-start | bytes 24968 | tf_op jit(solution)/shard_map/ppermute | solution.py:24
  46.5 3.6 collective-permute-start.2
  50.3 43.2 %gather_fusion.5 = f32[4096]{0:T(1024)} fusion(f32[32,128]{1,0:T(8,128)S(1)} %copy-done.1, s32[4096]{0:T(1024)S(1)} %fusion.156), kind=kCustom, calls=%fused_computation.5 | custom fusion | bytes 65536 | tf_op jit(solution)/shard_map/jvp(jit(take_along_axis))/gather | solution.py:71
  93.5 25.6 %gather_fusion.4 = f32[4096]{0:T(1024)S(1)} fusion(f32[32,128]{1,0:T(8,128)S(1)} %copy-done.2, s32[4096]{0:T(1024)S(1)} %fusion.156), kind=kCustom, calls=%fused_computation.4 | custom fusion | bytes 65536 | tf_op jit(solution)/shard_map/jvp(jit(take_along_axis))/gather | solution.py:71
  120.6 1.0 pad_maximum_fusion
  122.2 1.2 fusion.39
  127.1 1.0 pad_maximum_fusion.2
  129.3 8.6 %copy.109 = f32[3,2,128,128]{0,3,2,1:T(8,128)} copy(f32[3,2,128,128]{3,2,1,0:T(8,128)S(1)} %fusion.34) | data formatting | bytes 786432 | tf_op jit(solution)/shard_map/jvp()/sub | solution.py:163
  137.8 8.5 %copy.110 = f32[3,2,128,128]{0,3,2,1:T(8,128)} copy(f32[3,2,128,128]{3,2,1,0:T(8,128)S(1)} %get-tuple-element.106) | data formatting | bytes 786432 | tf_op jit(solution)/shard_map/jvp()/slice | solution.py:133
  146.3 16.5 %gather_fusion = f32[4096,3]{1,0:T(8,128)S(1)} fusion(f32[3,32768]{0,1:T(8,128)} %bitcast.416, s32[4096]{0:T(1024)S(1)} %get-tuple-element.69), kind=kCustom, calls=%fused_computation | custom fusion | bytes 114688 | tf_op jit(solution)/shard_map/jvp()/gather | solution.py:168
  162.9 40.6 %gather_fusion.3 = f32[4096]{0:T(1024)} fusion(f32[32768]{0:T(1024)S(1)} %bitcast.409, s32[4096]{0:T(1024)S(1)} %get-tuple-element.69), kind=kCustom, calls=%fused_computation.3 | custom fusion | bytes 49152 | tf_op jit(solution)/shard_map/jvp()/gather | solution.py:168
  203.5 23.0 %gather_fusion.1 = f32[4096]{0:T(1024)S(1)} fusion(f32[32768]{0:T(1024)S(1)} %bitcast.410, s32[4096]{0:T(1024)S(1)} %get-tuple-element.69), kind=kCustom, calls=%fused_computation.1 | custom fusion | bytes 49152 | tf_op jit(solution)/shard_map/jvp()/gather | solution.py:168
  226.5 36.5 %scatter_custom_fusion = f32[3,32768]{0,1:T(8,128)} fusion(f32[3,32768]{0,1:T(8,128)} %bitcast.411, s32[4096]{0:T(1024)} %bitcast.431, f32[4096,3]{1,0:T(8,128)S(1)} %gather_fusion, f32[4096]{0:T(1024)S(1)} %bitcast.421, f32[4096]{0:T(1024)S(1)} %bitcast.419), kind=kCustom, calls=%fused_computation.15 | custom fusion | flops 36864 | bytes 475136 | tf_op jit(solution)/shard_map/jvp()/scatter-add | solution.py:172
  263.0 10.7 %copy.115 = f32[3,2,128,128]{3,2,1,0:T(8,128)} copy(f32[3,2,128,128]{0,3,2,1:T(8,128)} %bitcast.412) | data formatting | bytes 786432
  273.7 2.5 fusion.31
  276.2 9.5 %copy.111 = f32[3,2,128,128]{0,3,2,1:T(8,128)} copy(f32[3,2,128,128]{3,2,1,0:T(8,128)} %fusion.31) | data formatting | bytes 786432 | tf_op jit(solution)/shard_map/jvp()/sub | solution.py:163
  285.7 8.5 %copy.112 = f32[3,2,128,128]{0,3,2,1:T(8,128)} copy(f32[3,2,128,128]{3,2,1,0:T(8,128)S(1)} %get-tuple-element.105) | data formatting | bytes 786432 | tf_op jit(solution)/shard_map/jvp()/slice | solution.py:133
  294.2 19.9 %gather_fusion.2 = f32[4096,3]{1,0:T(8,128)} fusion(f32[3,32768]{0,1:T(8,128)} %bitcast.417, s32[4096]{0:T(1024)S(1)} %get-tuple-element.69), kind=kCustom, calls=%fused_computation.2 | custom fusion | bytes 114688 | tf_op jit(solution)/shard_map/jvp()/gather | solution.py:168
  314.2 37.0 %scatter_custom_fusion.1 = f32[3,32768]{0,1:T(8,128)} fusion(f32[3,32768]{0,1:T(8,128)} %bitcast.413, s32[4096]{0:T(1024)} %bitcast.432, f32[4096,3]{1,0:T(8,128)} %gather_fusion.2, f32[4096,3]{1,0:T(8,128)S(1)} %gather_fusion, f32[4096]{0:T(1024)S(1)} %bitcast.427, f32[4096]{0:T(1024)S(1)} %bitcast.422, f32[4096]{0:T(1024)S(1)} %bitcast.420), kind=kCustom, calls=%fused_computation.13 | custom fusion | flops 73728 | bytes 2588672 | tf_op jit(solution)/shard_map/jvp()/scatter-add | solution.py:172
  351.1 10.6 %copy.116 = f32[3,2,128,128]{3,2,1,0:T(8,128)} copy(f32[3,2,128,128]{0,3,2,1:T(8,128)} %bitcast.414) | data formatting | bytes 786432
  361.8 4.6 add_reduce_fusion
  366.5 46.0 %all-reduce.4 = (f32[32,128]{1,0:T(8,128)S(1)}, f32[32,128]{1,0:T(8,128)S(1)}) all-reduce(f32[32,128]{1,0:T(8,128)S(1)} %get-tuple-element.55, f32[32,128]{1,0:T(8,128)S(1)} %get-tuple-element.54), channel_id=1, replica_groups=mesh['gx'=16,'gy'=16] {'gy'}, use_global_device_ids=true, to_apply=%region_3.4 | all-reduce | flops 8192 | bytes 65536 | tf_op jit(solution)/shard_map/psum | solution.py:201
  412.5 1.7 fusion.175
  414.3 1.7 fusion.174
  419.6 76.6 %psum.23 = f32[3,128]{1,0:T(4,128)} all-reduce(f32[3,128]{1,0:T(4,128)S(1)} %fusion.157), channel_id=1, replica_groups=mesh['gx'=16,'gy'=16] {'gx','gy'}, use_global_device_ids=true, to_apply=%region_9.10 | all-reduce | flops 384 | bytes 3072 | tf_op jit(solution)/shard_map/psum | solution.py:188
  (106 shorter events, 19.0 us)
Async XLA Ops:
  0.6 415.5 %copy-start = (f32[128]{0:T(128)S(1)}, f32[128]{0:T(128)}, u32[]{:S(2)}) copy-start(f32[128]{0:T(128)} %param.37) | copy-start | bytes 1540
  0.6 10.9 %copy-start.8 = (s32[32,128]{1,0:T(8,128)S(1)}, s32[32,128]{1,0:T(8,128)}, u32[]{:S(2)}) copy-start(s32[32,128]{1,0:T(8,128)} %param.29) | copy-start | bytes 49156
  0.7 11.5 %copy-start.12 = (f32[32,128]{1,0:T(8,128)S(1)}, f32[32,128]{1,0:T(8,128)}, u32[]{:S(2)}) copy-start(f32[32,128]{1,0:T(8,128)} %param.30) | copy-start | bytes 49156
  0.7 11.5 %copy-start.9 = (s32[32,128]{1,0:T(8,128)S(1)}, s32[32,128]{1,0:T(8,128)}, u32[]{:S(2)}) copy-start(s32[32,128]{1,0:T(8,128)} %param.31) | copy-start | bytes 49156
  5.6 31.5 %collective-permute-start.1 = (f32[8,2,1,128]{3,2,1,0:T(1,128)S(1)}, f32[8,2,1,128]{3,2,1,0:T(1,128)S(1)}, u32[]{:S(2)}, u32[]{:S(2)}) collective-permute-start(f32[8,2,1,128]{3,2,1,0:T(1,128)S(1)} %get-tuple-element.89), channel_id=1, source_target_pairs={{16,0},{32,16},{48,32},{64,48},{80,64},{96,80},{112,96},{128,112},... | collective-permute-start | bytes 24584 | tf_op jit(solution)/shard_map/ppermute | solution.py:24
  6.9 30.2 %collective-permute-start = (f32[8,2,1,128]{3,2,1,0:T(1,128)S(1)}, f32[8,2,1,128]{3,2,1,0:T(1,128)S(1)}, u32[]{:S(2)}, u32[]{:S(2)}) collective-permute-start(f32[8,2,1,128]{3,2,1,0:T(1,128)S(1)} %get-tuple-element.88), channel_id=1, source_target_pairs={{0,16},{16,32},{32,48},{48,64},{64,80},{80,96},{96,112},{112,128},... | collective-permute-start | bytes 24584 | tf_op jit(solution)/shard_map/ppermute | solution.py:23
  15.0 2.0 copy-start.16
  15.0 2.0 copy-start.19
  15.0 21.5 %copy-start.2 = (f32[32,128]{1,0:T(8,128)S(1)}, f32[32,128]{1,0:T(8,128)}, u32[]{:S(2)}) copy-start(f32[32,128]{1,0:T(8,128)} %param.27) | copy-start | bytes 49156
  37.6 12.6 %copy-start.1 = (f32[32,128]{1,0:T(8,128)S(1)}, f32[32,128]{1,0:T(8,128)}, u32[]{:S(2)}) copy-start(f32[32,128]{1,0:T(8,128)} %param.28) | copy-start | bytes 49156
  38.2 81.6 %collective-permute-start.3 = (f32[8,2,130,1]{2,0,3,1:T(8,128)S(1)}, f32[8,2,130,1]{2,0,3,1:T(8,128)S(1)}, u32[]{:S(2)}, u32[]{:S(2)}) collective-permute-start(f32[8,2,130,1]{2,0,3,1:T(8,128)S(1)} %copy.106), channel_id=1, source_target_pairs={{1,0},{2,1},{3,2},{4,3},{5,4},{6,5},{7,6},{8,7},{9,8},{10,9},{11,1... | collective-permute-start | bytes 24968 | tf_op jit(solution)/shard_map/ppermute | solution.py:24
  46.5 73.7 %collective-permute-start.2 = (f32[8,2,130,1]{2,0,3,1:T(8,128)S(1)}, f32[8,2,130,1]{2,0,3,1:T(8,128)S(1)}, u32[]{:S(2)}, u32[]{:S(2)}) collective-permute-start(f32[8,2,130,1]{2,0,3,1:T(8,128)S(1)} %copy.105), channel_id=1, source_target_pairs={{0,1},{1,2},{2,3},{3,4},{4,5},{5,6},{6,7},{7,8},{8,9},{9,10},{10,1... | collective-permute-start | bytes 24968 | tf_op jit(solution)/shard_map/ppermute | solution.py:23
  124.8 1.2 copy-start.5
  127.1 1.8 copy-start.6
  127.1 1.8 copy-start.7
  203.4 23.0 %copy-start.11 = (f32[4096]{0:T(1024)S(1)}, f32[4096]{0:T(1024)}, u32[]{:S(2)}) copy-start(f32[4096]{0:T(1024)} %gather_fusion.3) | copy-start | bytes 49156
  263.0 10.7 %copy-start.4 = (f32[3,1,128,128]{3,2,1,0:T(8,128)S(1)}, f32[3,1,128,128]{3,2,1,0:T(8,128)}, u32[]{:S(2)}) copy-start(f32[3,1,128,128]{3,2,1,0:T(8,128)} %get-tuple-element.112) | copy-start | bytes 589828
  361.8 50.7 %copy-start.3 = (bf16[32,128,128]{2,1,0:T(8,128)(2,1)S(1)}, bf16[32,128,128]{2,1,0:T(8,128)(2,1)}, u32[]{:S(2)}) copy-start(bf16[32,128,128]{2,1,0:T(8,128)(2,1)} %minimum_convert_fusion) | copy-start | bytes 3145732
  361.8 52.5 %copy-start.10 = (f32[4096]{0:T(1024)S(1)}, f32[4096]{0:T(1024)}, u32[]{:S(2)}) copy-start(f32[4096]{0:T(1024)} %gather_fusion.5) | copy-start | bytes 49156
  366.4 49.8 %copy-start.14 = (f32[32]{0:T(128)S(1)}, f32[32]{0:T(128)}, u32[]{:S(2)}) copy-start(f32[32]{0:T(128)} %slice_reduce_fusion.2) | copy-start | bytes 388
  366.4 49.8 %copy-start.15 = (s32[32]{0:T(128)S(1)}, s32[32]{0:T(128)}, u32[]{:S(2)}) copy-start(s32[32]{0:T(128)} %param.33) | copy-start | bytes 388
  366.4 49.8 %copy-start.17 = (f32[32]{0:T(128)S(1)}, f32[32]{0:T(128)}, u32[]{:S(2)}) copy-start(f32[32]{0:T(128)} %param.35) | copy-start | bytes 388
  366.4 49.8 %copy-start.18 = (f32[32]{0:T(128)S(1)}, f32[32]{0:T(128)}, u32[]{:S(2)}) copy-start(f32[32]{0:T(128)} %param.34) | copy-start | bytes 388
  366.4 49.8 %copy-start.20 = (s32[32,1]{0,1:T(1,128)S(1)}, s32[32,1]{0,1:T(1,128)}, u32[]{:S(2)}) copy-start(s32[32,1]{0,1:T(1,128)} %param.36) | copy-start | bytes 388
  366.5 49.8 %copy-start.21 = (f32[32]{0:T(128)S(1)}, f32[32]{0:T(128)}, u32[]{:S(2)}) copy-start(f32[32]{0:T(128)} %convolution_bitcast_fusion) | copy-start | bytes 388
  366.5 50.1 %copy-start.13 = (f32[32,128]{1,0:T(8,128)S(1)}, f32[32,128]{1,0:T(8,128)}, u32[]{:S(2)}) copy-start(f32[32,128]{1,0:T(8,128)} %param.32) | copy-start | bytes 49156
